TPU v7x, 32 devices: a whole 2x2x4 slice. The times are simulated.
32 devices in a mesh: gx: 4 (over y, core), gy: 4 (over z), gz: 2 (over x).
Axes of the slice: x: 2, y: 2, z: 4, core: 2. Of those that a mesh axis runs over, the one named last changes fastest.
Arguments:
- inputs: bfloat16 [64, 16, 32, 256], P(None, 'gx', 'gy', 'gz'), may hold values from -6 to 6
- weight: bfloat16 [4, 4, 4, 64, 32], replicated, may hold values from -0.25 to 0.25
- cotangent: bfloat16 [2, 2, 2, 32, 16, 32, 256], P(None, None, None, None, 'gx', 'gy', 'gz'), may hold values from -3 to 3
Outputs:
- upsampled: bfloat16 [2, 2, 2, 32, 16, 32, 256], P(None, None, None, None, 'gx', 'gy', 'gz')
- input_grad: bfloat16 [64, 16, 32, 256], P(None, 'gx', 'gy', 'gz')
- weight_grad: float32 [4, 4, 4, 64, 32], replicated
All inputs are finite; a program needn't handle non-finite values.
Results may differ from a plain program's by a relative error of at most 0.0018.
Values may be sent and summed in bfloat16 or wider, within the bound.
A program may use at most 192 MiB of HBM per device.

v0:
```python
import functools
import math

import jax
import jax.numpy as jnp
from jax import lax
from jax.experimental import pallas as pl
from jax.experimental.pallas import tpu as pltpu
from jax.sharding import PartitionSpec as P

TAPS = ((1, 3), (2, 0))
G_OFF = ((0, 1), (1, 0))
IN_SHIFT = ((0, -1), (0, 1))
PAIRS = [(p, h) for p in (0, 1) for h in (0, 1)]


def ring(value, axis, step):
    count = lax.axis_size(axis)
    return lax.ppermute(value, axis, [(i, (i + step) % count) for i in range(count)])


def line(value, axis, step):
    count = lax.axis_size(axis)
    pairs = [(i, i + step) for i in range(count) if 0 <= i + step < count]
    return lax.ppermute(value, axis, pairs)


def reorder(weight):
    for dim in range(3):
        parts = [lax.slice_in_dim(weight, k, k + 1, axis=dim) for k in (1, 3, 2, 0)]
        weight = jnp.concatenate(parts, axis=dim)
    return weight


def inverse_order(taps):
    for dim in range(3):
        parts = [lax.slice_in_dim(taps, k, k + 1, axis=dim) for k in (3, 0, 2, 1)]
        taps = jnp.concatenate(parts, axis=dim)
    return taps


def dot(a, b):
    return jnp.dot(a, b, preferred_element_type=jnp.float32)


def dot_nt(a, b):
    return lax.dot_general(a, b, (((1,), (1,)), ((), ())), preferred_element_type=jnp.float32)


def compute_kernel(in_ref, g_ref, zin_ref, zg_ref, wf_ref, wi_ref, up_ref, ig_ref, wg_ref):
    cells_x, cells_y, _, cells_z = ig_ref.shape
    in_ch = ig_ref.shape[2]
    out_ch = up_ref.shape[3] // 2
    wide = zin_ref.shape[-1]
    lane = lax.broadcasted_iota(jnp.int32, (in_ch, cells_z), 1)
    first = lane == 0
    last = lane == cells_z - 1

    def rolled(value, amount):
        return pltpu.roll(value, amount % value.shape[-1], 1)

    edge_up = []
    for px in (0, 1):
        for py in (0, 1):
            halves = []
            for pz in (0, 1):
                packed = zin_ref[pz].astype(jnp.float32)
                rows = []
                for hx in (0, 1):
                    for hy in (0, 1):
                        spot = (1 + IN_SHIFT[px][hx]) * (cells_y + 2) + 1 + IN_SHIFT[py][hy]
                        rows.append(rolled(packed, -spot))
                stacked = jnp.concatenate(rows, axis=0).astype(jnp.bfloat16)
                halves.append(
                    dot(wf_ref[px * 2 + py, pl.ds((2 * pz + 1) * out_ch, out_ch), :], stacked)
                )
            edge_up.append(halves)
    edge_ig = []
    for pz in (0, 1):
        rows = []
        for px, hx in PAIRS:
            for py, hy in PAIRS:
                packed = zg_ref[pz, px * 2 + py].astype(jnp.float32)
                spot = G_OFF[px][hx] * (cells_y + 1) + G_OFF[py][hy]
                rows.append(rolled(packed, -spot))
        stacked = jnp.concatenate(rows, axis=0).astype(jnp.bfloat16)
        edge_ig.append(dot(wi_ref[pz, in_ch : 2 * in_ch, :], stacked))

    wg_ref[...] = jnp.zeros_like(wg_ref)
    for x in range(cells_x):
        parts = [[], []]
        for pz in (0, 1):
            rows = []
            for px, hx in PAIRS:
                for py, hy in PAIRS:
                    rows.append(
                        jnp.concatenate(
                            [
                                g_ref[
                                    x + G_OFF[px][hx],
                                    y + G_OFF[py][hy],
                                    px * 2 + py,
                                    pl.ds(pz * out_ch, out_ch),
                                    :,
                                ]
                                for y in range(cells_y)
                            ],
                            axis=1,
                        )
                    )
            grads = jnp.concatenate(rows, axis=0)
            product = dot(wi_ref[pz], grads)
            shifted = []
            for y in range(cells_y):
                cols = slice(y * cells_z, (y + 1) * cells_z)
                spot = x * (cells_y + 1) + y
                if pz == 0:
                    far = rolled(product[in_ch:, cols], -1)
                    edge = rolled(edge_ig[0], cells_z - 1 - spot)
                    far = jnp.where(last, edge, far)
                else:
                    far = rolled(product[in_ch:, cols], 1)
                    edge = rolled(edge_ig[1], -spot)
                    far = jnp.where(first, edge, far)
                parts[pz].append(product[:in_ch, cols] + far)
                here = in_ref[x + 1, y + 1]
                packed = zin_ref[pz].astype(jnp.float32)
                spot = (x + 1) * (cells_y + 2) + y + 1
                if pz == 0:
                    near = jnp.where(
                        first, rolled(packed, -spot), rolled(here.astype(jnp.float32), 1)
                    )
                else:
                    near = jnp.where(
                        last,
                        rolled(packed, cells_z - 1 - spot),
                        rolled(here.astype(jnp.float32), -1),
                    )
                shifted.append(jnp.concatenate([here, near.astype(jnp.bfloat16)], axis=0))
            wg_ref[pz] += dot_nt(grads, jnp.concatenate(shifted, axis=1))
        for y in range(cells_y):
            ig_ref[x, y] = (parts[0][y] + parts[1][y]).astype(jnp.bfloat16)
        for px in (0, 1):
            for py in (0, 1):
                rows = []
                for hx in (0, 1):
                    for hy in (0, 1):
                        rows.append(
                            jnp.concatenate(
                                [
                                    in_ref[
                                        x + 1 + IN_SHIFT[px][hx], y + 1 + IN_SHIFT[py][hy]
                                    ]
                                    for y in range(cells_y)
                                ],
                                axis=1,
                            )
                        )
                product = dot(wf_ref[px * 2 + py], jnp.concatenate(rows, axis=0))
                for y in range(cells_y):
                    cols = slice(y * cells_z, (y + 1) * cells_z)
                    spot = x * (cells_y + 2) + y
                    edge0, edge1 = edge_up[px * 2 + py]
                    even = product[:out_ch, cols] + jnp.where(
                        first[:out_ch],
                        rolled(edge0, -spot),
                        rolled(product[out_ch : 2 * out_ch, cols], 1),
                    )
                    odd = product[2 * out_ch : 3 * out_ch, cols] + jnp.where(
                        last[:out_ch],
                        rolled(edge1, cells_z - 1 - spot),
                        rolled(product[3 * out_ch :, cols], -1),
                    )
                    up_ref[x, y, px * 2 + py, :out_ch] = even.astype(jnp.bfloat16)
                    up_ref[x, y, px * 2 + py, out_ch:] = odd.astype(jnp.bfloat16)


def packed_lanes(columns):
    count = columns.shape[0] * columns.shape[1]
    flat = jnp.moveaxis(columns.reshape((count,) + columns.shape[2:]), 0, -1)
    return jnp.pad(flat, [(0, 0)] * (flat.ndim - 1) + [(0, 128 - count)])


def body(inputs, weight, cotangent):
    in_ch, cells_x, cells_y, cells_z = inputs.shape
    out_ch = weight.shape[4]
    cells = inputs.transpose(1, 2, 0, 3)
    cells = jnp.concatenate([ring(cells[-1:], "gx", 1), cells, ring(cells[:1], "gx", -1)], axis=0)
    cells = jnp.concatenate(
        [ring(cells[:, -1:], "gy", 1), cells, ring(cells[:, :1], "gy", -1)], axis=1
    )
    grads = cotangent.transpose(4, 5, 0, 1, 2, 3, 6).reshape(
        (cells_x, cells_y, 2, 2, 2 * out_ch, cells_z)
    )
    grads = jnp.concatenate(
        [
            jnp.concatenate([grads[:, :, :1], ring(grads[:1, :, :1], "gx", -1)], axis=0),
            jnp.concatenate([ring(grads[-1:, :, 1:], "gx", 1), grads[:, :, 1:]], axis=0),
        ],
        axis=2,
    )
    grads = jnp.concatenate(
        [
            jnp.concatenate([grads[..., :1, :, :], ring(grads[:, :1, :, :1], "gy", -1)], axis=1),
            jnp.concatenate([ring(grads[:, -1:, :, 1:], "gy", 1), grads[..., 1:, :, :]], axis=1),
        ],
        axis=3,
    ).reshape((cells_x + 1, cells_y + 1, 4, 2 * out_ch, cells_z))
    z_in = jnp.stack(
        [
            line(packed_lanes(cells[..., -1]), "gz", 1),
            line(packed_lanes(cells[..., 0]), "gz", -1),
        ]
    )
    z_g = jnp.stack(
        [
            line(packed_lanes(grads[:, :, :, :out_ch, 0]), "gz", -1),
            line(packed_lanes(grads[:, :, :, out_ch:, -1]), "gz", 1),
        ]
    )
    taps = reorder(weight).reshape((2, 2, 2, 2, 2, 2, in_ch, out_ch))
    w_f = taps.transpose(0, 2, 4, 5, 7, 1, 3, 6).reshape((4, 4 * out_ch, 4 * in_ch))
    w_i = taps.transpose(4, 5, 6, 0, 1, 2, 3, 7).reshape((2, 2 * in_ch, 16 * out_ch))
    up, ig, wg = pl.pallas_call(
        compute_kernel,
        out_shape=(
            jax.ShapeDtypeStruct((cells_x, cells_y, 4, 2 * out_ch, cells_z), jnp.bfloat16),
            jax.ShapeDtypeStruct((cells_x, cells_y, in_ch, cells_z), jnp.bfloat16),
            jax.ShapeDtypeStruct((2, 16 * out_ch, 2 * in_ch), jnp.float32),
        ),
        in_specs=[pl.BlockSpec(memory_space=pltpu.VMEM)] * 6,
        out_specs=[pl.BlockSpec(memory_space=pltpu.VMEM)] * 3,
        compiler_params=pltpu.CompilerParams(vmem_limit_bytes=48 * 1024 * 1024),
    )(cells, grads, z_in, z_g, w_f, w_i)
    up = up.reshape((cells_x, cells_y, 2, 2, 2, out_ch, cells_z)).transpose(2, 3, 4, 5, 0, 1, 6)
    ig = ig.transpose(2, 0, 1, 3)
    total = lax.psum(wg, ("gx", "gy", "gz"))
    total = total.reshape((2, 2, 2, 2, 2, out_ch, 2, in_ch)).transpose(1, 2, 3, 4, 0, 6, 7, 5)
    total = inverse_order(total.reshape((4, 4, 4, in_ch, out_ch)))
    all_cells = (
        cells_x
        * lax.axis_size("gx")
        * cells_y
        * lax.axis_size("gy")
        * cells_z
        * lax.axis_size("gz")
    )
    return up, ig, total * (1.0 / math.sqrt(all_cells))


def solution(mesh):
    placed = (P(None, "gx", "gy", "gz"), P(), P(None, None, None, None, "gx", "gy", "gz"))
    return jax.shard_map(
        body,
        mesh=mesh,
        in_specs=placed,
        out_specs=(P(None, None, None, None, "gx", "gy", "gz"), P(None, "gx", "gy", "gz"), P()),
        check_vma=False,
    )
```

profile of v0, /device:TPU:0, one launch (start us, length us, event | category | flops | bytes accessed | tf_op | source)
XLA Modules:
  0.0 207.4 jit_solution(16844209098565836294)
XLA Ops:
  7.2 1.4 copy.46
  9.2 2.0 collective-permute-start.1
  11.2 1.1 fusion.2
  14.4 1.1 collective-permute-start.4
  15.5 1.4 fusion.1
  18.1 2.3 %collective-permute-start.2 = (bf16[6,1,64,128]{3,2,1,0:T(8,128)(2,1)}, bf16[6,1,64,128]{3,2,1,0:T(8,128)(2,1)}, u32[]{:S(2)}, u32[]{:S(2)}) collective-permute-start(bf16[6,1,64,128]{3,2,1,0:T(8,128)(2,1)} %get-tuple-element.39), channel_id=1, source_target_pairs={{0,2},{2,4},{4,6},{6,0},{1,3},{3,5},{5,7},{7,1},{8,10},{10,12},{12... | collective-permute-start | bytes 294920 | tf_op jit(solution)/shard_map/ppermute | solution.py:19
  20.4 2.0 collective-permute-start.3
  24.3 0.9 copy.31.wi_ref
  25.5 1.6 copy.38
  27.2 1.3 pad_maximum_fusion.2.in_ref
  28.6 1.4 slice_reduce_fusion.3
  30.2 1.3 collective-permute-start.9
  31.5 4.5 %collective-permute-start.8 = (bf16[64,128]{1,0:T(8,128)(2,1)S(1)}, bf16[64,128]{1,0:T(8,128)(2,1)S(1)}, u32[]{:S(2)}, u32[]{:S(2)}) collective-permute-start(bf16[64,128]{1,0:T(8,128)(2,1)S(1)} %pad.14), channel_id=1, source_target_pairs={{0,1},{2,3},{4,5},{6,7},{8,9},{10,11},{12,13},{14,15},{16,17},{18,... | collective-permute-start | bytes 49160 | tf_op jit(solution)/shard_map/ppermute | solution.py:25
  36.1 0.8 maximum_maximum_fusion.3
  36.9 2.4 %collective-permute-start.6 = (bf16[5,1,2,1,64,128]{5,4,3,2,1,0:T(8,128)(2,1)S(1)}, bf16[5,1,2,1,64,128]{5,4,3,2,1,0:T(8,128)(2,1)S(1)}, u32[]{:S(2)}, u32[]{:S(2)}) collective-permute-start(bf16[5,1,2,1,64,128]{5,4,3,2,1,0:T(8,128)(2,1)S(1)} %get-tuple-element.21), channel_id=1, source_target_pairs={{0,6},{2,0},{4,2},{6,4},{1,7},{3,1},{5,3},{7,5},{8,14},{10,8},{12,... | collective-permute-start | bytes 491528 | tf_op jit(solution)/shard_map/ppermute | solution.py:19
  39.3 1.3 maximum_maximum_fusion.1
  41.1 2.1 %collective-permute-done.6 = bf16[5,1,2,1,64,128]{5,4,3,2,1,0:T(8,128)(2,1)S(1)} collective-permute-done((bf16[5,1,2,1,64,128]{5,4,3,2,1,0:T(8,128)(2,1)S(1)}, bf16[5,1,2,1,64,128]{5,4,3,2,1,0:T(8,128)(2,1)S(1)}, u32[]{:S(2)}, u32[]{:S(2)}) %collective-permute-start.6) | collective-permute-done | bytes 163872 | tf_op jit(solution)/shard_map/ppermute | solution.py:19
  43.2 3.3 %collective-permute-done.7 = bf16[5,1,2,1,64,128]{5,4,3,2,1,0:T(8,128)(2,1)S(1)} collective-permute-done((bf16[5,1,2,1,64,128]{5,4,3,2,1,0:T(8,128)(2,1)S(1)}, bf16[5,1,2,1,64,128]{5,4,3,2,1,0:T(8,128)(2,1)S(1)}, u32[]{:S(2)}, u32[]{:S(2)}) %collective-permute-start.7) | collective-permute-done | bytes 163872 | tf_op jit(solution)/shard_map/ppermute | solution.py:19
  46.8 1.6 copy-done.4
  48.4 2.1 %slice_reduce_fusion.1 = (bf16[5,9,4,32]{3,2,1,0:T(4,128)(2,1)S(1)}, bf16[5,9,4,32]{3,2,1,0:T(4,128)(2,1)S(1)}) fusion(bf16[5,9,4,64,128]{4,3,2,1,0:T(8,128)(2,1)S(1)} %bitcast.35), kind=kLoop, calls=%fused_computation.4 | loop fusion | bytes 46080 | tf_op jit(solution)/shard_map/slice | solution.py:217
  50.8 1.4 collective-permute-start.11
  52.2 1.5 collective-permute-start.10
  53.7 4.2 %collective-permute-done.10 = bf16[4,32,128]{2,1,0:T(8,128)(2,1)S(1)} collective-permute-done((bf16[4,32,128]{2,1,0:T(8,128)(2,1)S(1)}, bf16[4,32,128]{2,1,0:T(8,128)(2,1)S(1)}, u32[]{:S(2)}, u32[]{:S(2)}) %collective-permute-start.10) | collective-permute-done | bytes 32800 | tf_op jit(solution)/shard_map/ppermute | solution.py:25
  58.0 0.9 copy-done
  58.9 6.7 %shard_map.58 = (bf16[4,8,4,64,128]{4,3,2,1,0:T(8,128)(2,1)S(1)}, bf16[4,8,64,128]{3,2,1,0:T(8,128)(2,1)S(1)}, f32[2,512,128]{2,1,0:T(8,128)S(1)}) custom-call(bf16[6,10,64,128]{3,2,1,0:T(8,128)(2,1)S(1)} %pad_maximum_fusion.2.in_ref, bf16[5,9,4,64,128]{4,3,2,1,0:T(8,128)(2,1)} %bitcast.36, bf16[2,64,128]{2,1,0:T(8,128)(2,1)S(1)} %pad_maximum_fusion.10.zin_ref, ...), custom_call_target="tpu_custom_call" | custom-call | tf_op jit(solution)/shard_map/pallas_call | solution.py:224
  67.2 1.6 reshape.36
  68.9 1.1 copy.33
  70.0 2.7 %copy.43 = bf16[4,8,2,2,2,32,128]{6,1,0,5,4,3,2:T(8,128)(2,1)} copy(bf16[4,8,2,2,2,32,128]{6,5,4,3,2,1,0:T(8,128)(2,1)S(1)} %bitcast.33) | data formatting | bytes 4194304 | tf_op jit(solution)/shard_map/reshape | solution.py:235
  72.7 1.1 copy.34
  73.8 123.9 %all-reduce.6.cloned.1.call-done = f32[4,4,4,64,32]{3,4,2,1,0:T(8,128)} async-done(((f32[4,4,4,64,32]{3,4,2,1,0:T(8,128)}), f32[4,4,4,64,32]{3,4,2,1,0:T(8,128)}) %all-reduce.6.cloned.1.call-update) | async-done | bytes 524304 | tf_op jit(solution)/shard_map/psum | solution.py:237
  197.7 1.3 fusion.5
  199.4 1.1 maximum_multiply_fusion
  (63 shorter events, 9.5 us)
Async XLA Ops:
  7.2 8.4 %copy-start.6 = (bf16[2,2,2,32,4,8,128]{6,5,4,3,2,1,0:T(8,128)(2,1)S(1)}, bf16[2,2,2,32,4,8,128]{6,5,4,3,2,1,0:T(8,128)(2,1)}, u32[]{:S(2)}) copy-start(bf16[2,2,2,32,4,8,128]{6,5,4,3,2,1,0:T(8,128)(2,1)} %param.5) | copy-start | bytes 6291460
  7.2 190.5 %all-reduce.6.cloned.1.call-start = ((), (), s32[]{:S(2)}) async-start(), calls=%async_computation | async-start | bytes 2097152 | tf_op jit(solution)/shard_map/psum | solution.py:237
  8.6 8.8 %copy-start.5 = (bf16[64,4,8,128]{3,0,2,1:T(8,128)(2,1)}, bf16[64,4,8,128]{3,0,2,1:T(8,128)(2,1)S(1)}, u32[]{:S(2)}) copy-start(bf16[64,4,8,128]{3,0,2,1:T(8,128)(2,1)S(1)} %copy.46) | copy-start | bytes 1572868
  8.6 8.7 %collective-permute-start = (bf16[1,8,64,128]{3,2,1,0:T(8,128)(2,1)S(1)}, bf16[1,8,64,128]{3,2,1,0:T(8,128)(2,1)S(1)}, u32[]{:S(2)}, u32[]{:S(2)}) collective-permute-start(bf16[1,8,64,128]{3,2,1,0:T(8,128)(2,1)S(1)} %get-tuple-element.53), channel_id=1, source_target_pairs={{0,8},{8,16},{16,24},{24,0},{1,9},{9,17},{17,25},{25,1},{2,10},{10... | collective-permute-start | bytes 393224 | tf_op jit(solution)/shard_map/ppermute | solution.py:19
  9.2 8.2 %collective-permute-start.1 = (bf16[1,8,64,128]{3,2,1,0:T(8,128)(2,1)S(1)}, bf16[1,8,64,128]{3,2,1,0:T(8,128)(2,1)S(1)}, u32[]{:S(2)}, u32[]{:S(2)}) collective-permute-start(bf16[1,8,64,128]{3,2,1,0:T(8,128)(2,1)S(1)} %get-tuple-element.54), channel_id=1, source_target_pairs={{0,24},{8,0},{16,8},{24,16},{1,25},{9,1},{17,9},{25,17},{2,26},{10... | collective-permute-start | bytes 393224 | tf_op jit(solution)/shard_map/ppermute | solution.py:19
  12.3 4.7 %copy-start.7 = (bf16[4,4,4,64,32]{3,4,2,1,0:T(8,128)(2,1)S(1)}, bf16[4,4,4,64,32]{3,4,2,1,0:T(8,128)(2,1)}, u32[]{:S(2)}) copy-start(bf16[4,4,4,64,32]{3,4,2,1,0:T(8,128)(2,1)} %param.4) | copy-start | bytes 786436
  13.0 23.1 %collective-permute-start.5 = (bf16[1,8,1,2,64,128]{5,4,3,2,1,0:T(8,128)(2,1)}, bf16[1,8,1,2,64,128]{5,4,3,2,1,0:T(8,128)(2,1)}, u32[]{:S(2)}, u32[]{:S(2)}) collective-permute-start(bf16[1,8,1,2,64,128]{5,4,3,2,1,0:T(8,128)(2,1)} %copy.37), channel_id=1, source_target_pairs={{0,8},{8,16},{16,24},{24,0},{1,9},{9,17},{17,25},{25,1},{2,10},{10... | collective-permute-start | bytes 786440 | tf_op jit(solution)/shard_map/ppermute | solution.py:19
  14.4 21.7 %collective-permute-start.4 = (bf16[1,8,1,2,64,128]{5,4,3,2,1,0:T(8,128)(2,1)}, bf16[1,8,1,2,64,128]{5,4,3,2,1,0:T(8,128)(2,1)}, u32[]{:S(2)}, u32[]{:S(2)}) collective-permute-start(bf16[1,8,1,2,64,128]{5,4,3,2,1,0:T(8,128)(2,1)} %copy.36), channel_id=1, source_target_pairs={{0,24},{8,0},{16,8},{24,16},{1,25},{9,1},{17,9},{25,17},{2,26},{10... | collective-permute-start | bytes 786440 | tf_op jit(solution)/shard_map/ppermute | solution.py:19
  17.4 6.3 %copy-start.8 = (bf16[1,8,64,128]{3,2,1,0:T(8,128)(2,1)}, bf16[1,8,64,128]{3,2,1,0:T(8,128)(2,1)S(1)}, u32[]{:S(2)}) copy-start(bf16[1,8,64,128]{3,2,1,0:T(8,128)(2,1)S(1)} %collective-permute-done.1) | copy-start | bytes 393220
  18.1 9.0 %collective-permute-start.2 = (bf16[6,1,64,128]{3,2,1,0:T(8,128)(2,1)}, bf16[6,1,64,128]{3,2,1,0:T(8,128)(2,1)}, u32[]{:S(2)}, u32[]{:S(2)}) collective-permute-start(bf16[6,1,64,128]{3,2,1,0:T(8,128)(2,1)} %get-tuple-element.39), channel_id=1, source_target_pairs={{0,2},{2,4},{4,6},{6,0},{1,3},{3,5},{5,7},{7,1},{8,10},{10,12},{12... | collective-permute-start | bytes 294920 | tf_op jit(solution)/shard_map/ppermute | solution.py:19
  20.4 6.7 %collective-permute-start.3 = (bf16[6,1,64,128]{3,2,1,0:T(8,128)(2,1)}, bf16[6,1,64,128]{3,2,1,0:T(8,128)(2,1)}, u32[]{:S(2)}, u32[]{:S(2)}) collective-permute-start(bf16[6,1,64,128]{3,2,1,0:T(8,128)(2,1)} %get-tuple-element.40), channel_id=1, source_target_pairs={{0,6},{2,0},{4,2},{6,4},{1,7},{3,1},{5,3},{7,5},{8,14},{10,8},{12,... | collective-permute-start | bytes 294920 | tf_op jit(solution)/shard_map/ppermute | solution.py:19
  30.2 23.4 %collective-permute-start.9 = (bf16[64,128]{1,0:T(8,128)(2,1)S(1)}, bf16[64,128]{1,0:T(8,128)(2,1)S(1)}, u32[]{:S(2)}, u32[]{:S(2)}) collective-permute-start(bf16[64,128]{1,0:T(8,128)(2,1)S(1)} %pad.15), channel_id=1, source_target_pairs={{1,0},{3,2},{5,4},{7,6},{9,8},{11,10},{13,12},{15,14},{17,16},{19,... | collective-permute-start | bytes 49160 | tf_op jit(solution)/shard_map/ppermute | solution.py:25
  31.5 22.1 %collective-permute-start.8 = (bf16[64,128]{1,0:T(8,128)(2,1)S(1)}, bf16[64,128]{1,0:T(8,128)(2,1)S(1)}, u32[]{:S(2)}, u32[]{:S(2)}) collective-permute-start(bf16[64,128]{1,0:T(8,128)(2,1)S(1)} %pad.14), channel_id=1, source_target_pairs={{0,1},{2,3},{4,5},{6,7},{8,9},{10,11},{12,13},{14,15},{16,17},{18,... | collective-permute-start | bytes 49160 | tf_op jit(solution)/shard_map/ppermute | solution.py:25
  36.9 6.3 %collective-permute-start.6 = (bf16[5,1,2,1,64,128]{5,4,3,2,1,0:T(8,128)(2,1)S(1)}, bf16[5,1,2,1,64,128]{5,4,3,2,1,0:T(8,128)(2,1)S(1)}, u32[]{:S(2)}, u32[]{:S(2)}) collective-permute-start(bf16[5,1,2,1,64,128]{5,4,3,2,1,0:T(8,128)(2,1)S(1)} %get-tuple-element.21), channel_id=1, source_target_pairs={{0,6},{2,0},{4,2},{6,4},{1,7},{3,1},{5,3},{7,5},{8,14},{10,8},{12,... | collective-permute-start | bytes 491528 | tf_op jit(solution)/shard_map/ppermute | solution.py:19
  39.3 7.3 %collective-permute-start.7 = (bf16[5,1,2,1,64,128]{5,4,3,2,1,0:T(8,128)(2,1)S(1)}, bf16[5,1,2,1,64,128]{5,4,3,2,1,0:T(8,128)(2,1)S(1)}, u32[]{:S(2)}, u32[]{:S(2)}) collective-permute-start(bf16[5,1,2,1,64,128]{5,4,3,2,1,0:T(8,128)(2,1)S(1)} %get-tuple-element.22), channel_id=1, source_target_pairs={{0,2},{2,4},{4,6},{6,0},{1,3},{3,5},{5,7},{7,1},{8,10},{10,12},{12... | collective-permute-start | bytes 491528 | tf_op jit(solution)/shard_map/ppermute | solution.py:19
  46.8 1.6 copy-start.4
  50.8 2.9 %collective-permute-start.11 = (bf16[4,32,128]{2,1,0:T(8,128)(2,1)S(1)}, bf16[4,32,128]{2,1,0:T(8,128)(2,1)S(1)}, u32[]{:S(2)}, u32[]{:S(2)}) collective-permute-start(bf16[4,32,128]{2,1,0:T(8,128)(2,1)S(1)} %pad.17), channel_id=1, source_target_pairs={{0,1},{2,3},{4,5},{6,7},{8,9},{10,11},{12,13},{14,15},{16,17},{18,... | collective-permute-start | bytes 98312 | tf_op jit(solution)/shard_map/ppermute | solution.py:25
  52.2 5.8 %collective-permute-start.10 = (bf16[4,32,128]{2,1,0:T(8,128)(2,1)S(1)}, bf16[4,32,128]{2,1,0:T(8,128)(2,1)S(1)}, u32[]{:S(2)}, u32[]{:S(2)}) collective-permute-start(bf16[4,32,128]{2,1,0:T(8,128)(2,1)S(1)} %pad.16), channel_id=1, source_target_pairs={{1,0},{3,2},{5,4},{7,6},{9,8},{11,10},{13,12},{15,14},{17,16},{19,... | collective-permute-start | bytes 98312 | tf_op jit(solution)/shard_map/ppermute | solution.py:25
  58.0 1.0 copy-start
  65.6 0.8 copy-start.1
  66.4 0.8 copy-start.2
  70.0 2.7 %copy-start.3 = (bf16[4,8,64,128]{3,2,1,0:T(8,128)(2,1)S(1)}, bf16[4,8,64,128]{3,2,1,0:T(8,128)(2,1)}, u32[]{:S(2)}) copy-start(bf16[4,8,64,128]{3,2,1,0:T(8,128)(2,1)} %copy-done.2) | copy-start | bytes 1572868
Sparse Core Ops, SparseCore 0:
  70.1 127.5 all-reduce.5
where the time goes:
time: 208 us; the launch traced here: 207 us
  waiting for transfers between devices  134 us (64%)
  local copies, waits for them, and re-layouts  26.8 us (13%)
  starting transfers between devices  19.7 us (9%)
  between operations  14.4 us (7%)
  Pallas kernels  6.68 us (3%)
  other arithmetic  6.22 us (3%)
    psum x1, waiting for transfers between devices, body(): total = lax.psum(wg, ('gx', 'gy', 'gz'))  124 us
    ppermute x8, starting transfers between devices, ring(): lax.ppermute(value, axis, [(i, (i + step) % count) for i in range(count)])  11 us
    unnamed x24, local copies, waits for them, and re-layouts  10.2 us
    ppermute x4, starting transfers between devices, line(): return lax.ppermute(value, axis, pairs)  8.66 us
    pallas_call x1, Pallas kernels, body(): pl.pallas_call(compute_kernel, out_shape=(jax.ShapeDtypeStruct((cells_x,...  6.68 us
    ppermute x8, waiting for transfers between devices, ring(): lax.ppermute(value, axis, [(i, (i + step) % count) for i in range(count)])  5.43 us
    ppermute x4, waiting for transfers between devices, line(): return lax.ppermute(value, axis, pairs)  4.3 us
  transfers between devices with their start and end apart: 13, of which 5 were waited for; matrix products, arithmetic and copies ran while one was open for 11% of the time, Pallas kernels for 0%

commit v1 on v0

--- a/solution.py
+++ b/solution.py
@@ -14,29 +14,7 @@
 PAIRS = [(p, h) for p in (0, 1) for h in (0, 1)]
 
 
-def ring(value, axis, step):
-    count = lax.axis_size(axis)
-    return lax.ppermute(value, axis, [(i, (i + step) % count) for i in range(count)])
-
-
-def line(value, axis, step):
-    count = lax.axis_size(axis)
-    pairs = [(i, i + step) for i in range(count) if 0 <= i + step < count]
-    return lax.ppermute(value, axis, pairs)
-
-
-def reorder(weight):
-    for dim in range(3):
-        parts = [lax.slice_in_dim(weight, k, k + 1, axis=dim) for k in (1, 3, 2, 0)]
-        weight = jnp.concatenate(parts, axis=dim)
-    return weight
-
-
-def inverse_order(taps):
-    for dim in range(3):
-        parts = [lax.slice_in_dim(taps, k, k + 1, axis=dim) for k in (3, 0, 2, 1)]
-        taps = jnp.concatenate(parts, axis=dim)
-    return taps
+MESH = pl.DeviceIdType.MESH
 
 
 def dot(a, b):
@@ -47,7 +25,9 @@
     return lax.dot_general(a, b, (((1,), (1,)), ((), ())), preferred_element_type=jnp.float32)
 
 
-def compute_kernel(in_ref, g_ref, zin_ref, zg_ref, wf_ref, wi_ref, up_ref, ig_ref, wg_ref):
+def compute_kernel(
+    in_ref, g_ref, zin_ref, zg_ref, w_ref, up_ref, ig_ref, wg_ref, wf_ref, wi_ref
+):
     cells_x, cells_y, _, cells_z = ig_ref.shape
     in_ch = ig_ref.shape[2]
     out_ch = up_ref.shape[3] // 2
@@ -58,6 +38,28 @@
 
     def rolled(value, amount):
         return pltpu.roll(value, amount % value.shape[-1], 1)
+
+    for px in (0, 1):
+        for py in (0, 1):
+            for pz, hz in PAIRS:
+                wf_ref[px * 2 + py, pl.ds((2 * pz + hz) * out_ch, out_ch), :] = jnp.concatenate(
+                    [
+                        w_ref[TAPS[px][hx], TAPS[py][hy], TAPS[pz][hz]]
+                        for hx in (0, 1)
+                        for hy in (0, 1)
+                    ],
+                    axis=1,
+                )
+    for pz in (0, 1):
+        rows = [
+            jnp.concatenate(
+                [w_ref[TAPS[px][hx], TAPS[py][hy], TAPS[pz][hz]] for hz in (0, 1)], axis=1
+            )
+            for px, hx in PAIRS
+            for py, hy in PAIRS
+        ]
+        stacked = jnp.concatenate(rows, axis=0).astype(jnp.float32)
+        wi_ref[pz] = stacked.T.astype(jnp.bfloat16)
 
     edge_up = []
     for px in (0, 1):
@@ -175,52 +177,297 @@
                     up_ref[x, y, px * 2 + py, out_ch:] = odd.astype(jnp.bfloat16)
 
 
-def packed_lanes(columns):
-    count = columns.shape[0] * columns.shape[1]
-    flat = jnp.moveaxis(columns.reshape((count,) + columns.shape[2:]), 0, -1)
-    return jnp.pad(flat, [(0, 0)] * (flat.ndim - 1) + [(0, 128 - count)])
+def halo_kernel(
+    in_ref,
+    g_ref,
+    ext_ref,
+    gext_ref,
+    zin_ref,
+    zg_ref,
+    pack_in,
+    pack_g,
+    face_in,
+    face_g,
+    send_sem,
+    recv_sem,
+):
+    cells_x, cells_y, in_ch, cells_z = in_ref.shape
+    out_ch = g_ref.shape[3] // 2
+    count_x, count_y = lax.axis_size("gx"), lax.axis_size("gy")
+    me_x, me_y, me_z = lax.axis_index("gx"), lax.axis_index("gy"), lax.axis_index("gz")
+    right_x = {"gx": lax.rem(me_x + 1, count_x)}
+    left_x = {"gx": lax.rem(me_x + count_x - 1, count_x)}
+    right_y = {"gy": lax.rem(me_y + 1, count_y)}
+    left_y = {"gy": lax.rem(me_y + count_y - 1, count_y)}
+    other_z = {"gz": 1 - me_z}
+    barrier = pltpu.get_barrier_semaphore()
+    for neighbour in (right_x, left_x, right_y, left_y, other_z):
+        pl.semaphore_signal(barrier, inc=1, device_id=neighbour, device_id_type=MESH)
+    pl.semaphore_wait(barrier, 5)
+
+    used = [0]
+
+    def send(src, dst, device):
+        n = used[0]
+        used[0] += 1
+        copy = pltpu.make_async_remote_copy(
+            src_ref=src,
+            dst_ref=dst,
+            send_sem=send_sem.at[n],
+            recv_sem=recv_sem.at[n],
+            device_id=device,
+            device_id_type=MESH,
+        )
+        copy.start()
+        return copy
+
+    inner_x, inner_y = pl.ds(1, cells_x), pl.ds(1, cells_y)
+    over_x = [
+        send(in_ref.at[cells_x - 1], ext_ref.at[0, inner_y], right_x),
+        send(in_ref.at[0], ext_ref.at[cells_x + 1, inner_y], left_x),
+    ]
+    over_y = [
+        send(in_ref.at[:, cells_y - 1], ext_ref.at[inner_x, 0], right_y),
+        send(in_ref.at[:, 0], ext_ref.at[inner_x, cells_y + 1], left_y),
+    ]
+    for px in (0, 1):
+        for py in (0, 1):
+            n = px * 2 + py
+            own_x, own_y = pl.ds(px, cells_x), pl.ds(py, cells_y)
+            if px == 0:
+                over_x.append(send(g_ref.at[0, :, n], gext_ref.at[cells_x, own_y, n], left_x))
+            else:
+                over_x.append(send(g_ref.at[cells_x - 1, :, n], gext_ref.at[0, own_y, n], right_x))
+            if py == 0:
+                over_y.append(send(g_ref.at[:, 0, n], gext_ref.at[own_x, cells_y, n], left_y))
+            else:
+                over_y.append(send(g_ref.at[:, cells_y - 1, n], gext_ref.at[own_x, 0, n], right_y))
+
+    ext_ref[1 : cells_x + 1, 1 : cells_y + 1] = in_ref[...]
+    for px in (0, 1):
+        for py in (0, 1):
+            n = px * 2 + py
+            gext_ref[px : px + cells_x, py : py + cells_y, n] = g_ref[:, :, n]
+    zin_ref[me_z] = jnp.zeros_like(zin_ref[0])
+    zg_ref[1 - me_z] = jnp.zeros_like(zg_ref[0])
+
+    wide = zin_ref.shape[-1]
+    source = (1 - me_z) * (cells_z - 1)
+    half = pl.ds(pl.multiple_of((1 - me_z) * out_ch, out_ch), out_ch)
+
+    def pack(dst, load, spot_of, count, stride):
+        lane = lax.broadcasted_iota(jnp.int32, dst.shape, 1)
+
+        def step(i, held):
+            x, y = spot_of(i)
+            spot = x * stride + y
+            value = load(x, y).astype(jnp.float32)
+            turned = pltpu.roll(value, lax.rem(spot + wide - source, wide), 1)
+            return jnp.where(lane == spot, turned, held)
+
+        dst[...] = lax.fori_loop(0, count, step, dst[...])
+
+    def load_in(x, y):
+        return ext_ref[x, y]
+
+    def load_g(x, y):
+        return gext_ref[x, y, :, half, :].reshape((4 * out_ch, cells_z))
+
+    pack_in[...] = jnp.zeros_like(pack_in)
+    pack_g[...] = jnp.zeros_like(pack_g)
+    row = cells_y + 2
+    pack(pack_in, load_in, lambda i: (1 + i // cells_y, 1 + i % cells_y), cells_x * cells_y, row)
+    pack(
+        pack_g,
+        load_g,
+        lambda i: (1 + i // (cells_y - 1), 1 + i % (cells_y - 1)),
+        (cells_x - 1) * (cells_y - 1),
+        row - 1,
+    )
+
+    for copy in over_x:
+        copy.wait()
+    corners = [
+        send(ext_ref.at[0, cells_y], ext_ref.at[0, 0], right_y),
+        send(ext_ref.at[cells_x + 1, cells_y], ext_ref.at[cells_x + 1, 0], right_y),
+        send(ext_ref.at[0, 1], ext_ref.at[0, cells_y + 1], left_y),
+        send(ext_ref.at[cells_x + 1, 1], ext_ref.at[cells_x + 1, cells_y + 1], left_y),
+    ]
+    for px in (0, 1):
+        far = cells_x if px == 0 else 0
+        n = px * 2
+        corners.append(send(gext_ref.at[far, 0, n], gext_ref.at[far, cells_y, n], left_y))
+        corners.append(send(gext_ref.at[far, cells_y, n + 1], gext_ref.at[far, 0, n + 1], right_y))
+    for copy in over_y:
+        copy.wait()
+    pack(
+        pack_in,
+        load_in,
+        lambda i: (1 + i // 2, (i % 2) * (cells_y + 1)),
+        2 * cells_x,
+        row,
+    )
+    pack(
+        pack_g,
+        load_g,
+        lambda i: (1 + i // 2, (i % 2) * cells_y),
+        2 * (cells_x - 1),
+        row - 1,
+    )
+    for copy in corners:
+        copy.wait()
+    pack(
+        pack_in,
+        load_in,
+        lambda i: ((i % 2) * (cells_x + 1), i // 2),
+        2 * (cells_y + 2),
+        row,
+    )
+    pack(
+        pack_g,
+        load_g,
+        lambda i: ((i % 2) * cells_x, i // 2),
+        2 * (cells_y + 1),
+        row - 1,
+    )
+    face_in[...] = pack_in[...].astype(jnp.bfloat16)
+    face_g[...] = pack_g[...].astype(jnp.bfloat16)
+    over_z = [
+        send(face_in, zin_ref.at[me_z], other_z),
+        send(face_g, zg_ref.at[1 - me_z], other_z),
+    ]
+    for copy in over_z:
+        copy.wait()
+
+
+def reduce_kernel(
+    streams, factor, part_ref, out_ref, total, landed, gathered, send_sem, recv_sem
+):
+    rows = part_ref.shape[0]
+    each = rows // len(streams)
+    steps = len(streams[0])
+    place = {}
+    for axis, bit in streams[0]:
+        me = lax.axis_index(axis)
+        side = lax.rem(lax.div(me, bit), 2)
+        place[axis, bit] = (side, {axis: me + bit - 2 * bit * side})
+
+    barrier = pltpu.get_barrier_semaphore()
+    for side, partner in place.values():
+        pl.semaphore_signal(barrier, inc=1, device_id=partner, device_id_type=MESH)
+    pl.semaphore_wait(barrier, steps)
+
+    total[...] = part_ref[...]
+
+    def copy(src, dst, n, partner):
+        made = pltpu.make_async_remote_copy(
+            src_ref=src,
+            dst_ref=dst,
+            send_sem=send_sem.at[n],
+            recv_sem=recv_sem.at[n],
+            device_id=partner,
+            device_id_type=MESH,
+        )
+        made.start()
+        return made
+
+    starts = [j * each for j in range(len(streams))]
+    kept = [[] for _ in streams]
+    for step in range(steps):
+        size = each >> (step + 1)
+        flying = []
+        for j, order in enumerate(streams):
+            side, partner = place[order[step]]
+            keep = pl.multiple_of(starts[j] + side * size, 8)
+            give = pl.multiple_of(starts[j] + (1 - side) * size, 8)
+            area = pl.ds(j * each + each - 2 * size, size)
+            flying.append(
+                copy(
+                    total.at[pl.ds(give, size)],
+                    landed.at[area],
+                    j * steps + step,
+                    partner,
+                )
+            )
+            starts[j] = keep
+            kept[j].append(keep)
+        for j in range(len(streams)):
+            flying[j].wait()
+            area = pl.ds(j * each + each - 2 * size, size)
+            mine = pl.ds(starts[j], size)
+            total[mine, :] = total[mine, :] + landed[area, :]
+    for j in range(len(streams)):
+        mine = pl.ds(starts[j], each >> steps)
+        gathered[mine, :] = total[mine, :]
+    base = len(streams) * steps
+    for step in reversed(range(steps)):
+        size = each >> (step + 1)
+        flying = []
+        for j, order in enumerate(streams):
+            partner = place[order[step]][1]
+            mine = pl.ds(kept[j][step], size)
+            flying.append(
+                copy(gathered.at[mine], gathered.at[mine], base + j * steps + step, partner)
+            )
+        for made in flying:
+            made.wait()
+
+    out_ch, in_ch = out_ref.shape[3:]
+    for pz in (0, 1):
+        for a, (px, hx) in enumerate(PAIRS):
+            for b, (py, hy) in enumerate(PAIRS):
+                block = gathered[pl.ds(((pz * 4 + a) * 4 + b) * out_ch, out_ch), :] * factor
+                for hz in (0, 1):
+                    out_ref[TAPS[px][hx], TAPS[py][hy], TAPS[pz][hz]] = block[
+                        :, hz * in_ch : (hz + 1) * in_ch
+                    ]
+
+
+def reduce_plan(rows):
+    sizes = {axis: lax.axis_size(axis) for axis in ("gz", "gx", "gy")}
+    rest = [
+        (axis, 1 << bit)
+        for axis, size in sizes.items()
+        for bit in range(size.bit_length() - 1)
+        if (axis, bit) != ("gx", 0)
+    ]
+    devices = math.prod(sizes.values())
+    count = max(1, min(len(rest), rows // (8 * devices)))
+    streams = [[("gx", 1)] + rest[j:] + rest[:j] for j in range(count)]
+    return streams
 
 
 def body(inputs, weight, cotangent):
     in_ch, cells_x, cells_y, cells_z = inputs.shape
     out_ch = weight.shape[4]
     cells = inputs.transpose(1, 2, 0, 3)
-    cells = jnp.concatenate([ring(cells[-1:], "gx", 1), cells, ring(cells[:1], "gx", -1)], axis=0)
-    cells = jnp.concatenate(
-        [ring(cells[:, -1:], "gy", 1), cells, ring(cells[:, :1], "gy", -1)], axis=1
-    )
     grads = cotangent.transpose(4, 5, 0, 1, 2, 3, 6).reshape(
-        (cells_x, cells_y, 2, 2, 2 * out_ch, cells_z)
-    )
-    grads = jnp.concatenate(
-        [
-            jnp.concatenate([grads[:, :, :1], ring(grads[:1, :, :1], "gx", -1)], axis=0),
-            jnp.concatenate([ring(grads[-1:, :, 1:], "gx", 1), grads[:, :, 1:]], axis=0),
+        (cells_x, cells_y, 4, 2 * out_ch, cells_z)
+    )
+    taps = weight.transpose(0, 1, 2, 4, 3)
+    vmem = pl.BlockSpec(memory_space=pltpu.VMEM)
+    cells, grads, z_in, z_g = pl.pallas_call(
+        halo_kernel,
+        out_shape=(
+            jax.ShapeDtypeStruct((cells_x + 2, cells_y + 2, in_ch, cells_z), jnp.bfloat16),
+            jax.ShapeDtypeStruct((cells_x + 1, cells_y + 1, 4, 2 * out_ch, cells_z), jnp.bfloat16),
+            jax.ShapeDtypeStruct((2, in_ch, 128), jnp.bfloat16),
+            jax.ShapeDtypeStruct((2, 4 * out_ch, 128), jnp.bfloat16),
+        ),
+        in_specs=[vmem] * 2,
+        out_specs=[vmem] * 4,
+        scratch_shapes=[
+            pltpu.VMEM((in_ch, 128), jnp.float32),
+            pltpu.VMEM((4 * out_ch, 128), jnp.float32),
+            pltpu.VMEM((in_ch, 128), jnp.bfloat16),
+            pltpu.VMEM((4 * out_ch, 128), jnp.bfloat16),
+            pltpu.SemaphoreType.DMA((22,)),
+            pltpu.SemaphoreType.DMA((22,)),
         ],
-        axis=2,
-    )
-    grads = jnp.concatenate(
-        [
-            jnp.concatenate([grads[..., :1, :, :], ring(grads[:, :1, :, :1], "gy", -1)], axis=1),
-            jnp.concatenate([ring(grads[:, -1:, :, 1:], "gy", 1), grads[..., 1:, :, :]], axis=1),
-        ],
-        axis=3,
-    ).reshape((cells_x + 1, cells_y + 1, 4, 2 * out_ch, cells_z))
-    z_in = jnp.stack(
-        [
-            line(packed_lanes(cells[..., -1]), "gz", 1),
-            line(packed_lanes(cells[..., 0]), "gz", -1),
-        ]
-    )
-    z_g = jnp.stack(
-        [
-            line(packed_lanes(grads[:, :, :, :out_ch, 0]), "gz", -1),
-            line(packed_lanes(grads[:, :, :, out_ch:, -1]), "gz", 1),
-        ]
-    )
-    taps = reorder(weight).reshape((2, 2, 2, 2, 2, 2, in_ch, out_ch))
-    w_f = taps.transpose(0, 2, 4, 5, 7, 1, 3, 6).reshape((4, 4 * out_ch, 4 * in_ch))
-    w_i = taps.transpose(4, 5, 6, 0, 1, 2, 3, 7).reshape((2, 2 * in_ch, 16 * out_ch))
+        compiler_params=pltpu.CompilerParams(
+            collective_id=0, has_side_effects=True, vmem_limit_bytes=48 * 1024 * 1024
+        ),
+    )(cells, grads)
     up, ig, wg = pl.pallas_call(
         compute_kernel,
         out_shape=(
@@ -228,15 +475,16 @@
             jax.ShapeDtypeStruct((cells_x, cells_y, in_ch, cells_z), jnp.bfloat16),
             jax.ShapeDtypeStruct((2, 16 * out_ch, 2 * in_ch), jnp.float32),
         ),
-        in_specs=[pl.BlockSpec(memory_space=pltpu.VMEM)] * 6,
-        out_specs=[pl.BlockSpec(memory_space=pltpu.VMEM)] * 3,
+        in_specs=[vmem] * 5,
+        out_specs=[vmem] * 3,
+        scratch_shapes=[
+            pltpu.VMEM((4, 4 * out_ch, 4 * in_ch), jnp.bfloat16),
+            pltpu.VMEM((2, 2 * in_ch, 16 * out_ch), jnp.bfloat16),
+        ],
         compiler_params=pltpu.CompilerParams(vmem_limit_bytes=48 * 1024 * 1024),
-    )(cells, grads, z_in, z_g, w_f, w_i)
+    )(cells, grads, z_in, z_g.reshape((2, 4, out_ch, 128)), taps)
     up = up.reshape((cells_x, cells_y, 2, 2, 2, out_ch, cells_z)).transpose(2, 3, 4, 5, 0, 1, 6)
     ig = ig.transpose(2, 0, 1, 3)
-    total = lax.psum(wg, ("gx", "gy", "gz"))
-    total = total.reshape((2, 2, 2, 2, 2, out_ch, 2, in_ch)).transpose(1, 2, 3, 4, 0, 6, 7, 5)
-    total = inverse_order(total.reshape((4, 4, 4, in_ch, out_ch)))
     all_cells = (
         cells_x
         * lax.axis_size("gx")
@@ -245,7 +493,26 @@
         * cells_z
         * lax.axis_size("gz")
     )
-    return up, ig, total * (1.0 / math.sqrt(all_cells))
+    rows = 32 * out_ch
+    plan = reduce_plan(rows)
+    copies = 2 * len(plan) * len(plan[0])
+    total = pl.pallas_call(
+        functools.partial(reduce_kernel, plan, 1.0 / math.sqrt(all_cells)),
+        out_shape=jax.ShapeDtypeStruct((4, 4, 4, out_ch, in_ch), jnp.float32),
+        in_specs=[vmem],
+        out_specs=vmem,
+        scratch_shapes=[
+            pltpu.VMEM((rows, 2 * in_ch), jnp.float32),
+            pltpu.VMEM((rows, 2 * in_ch), jnp.float32),
+            pltpu.VMEM((rows, 2 * in_ch), jnp.float32),
+            pltpu.SemaphoreType.DMA((copies,)),
+            pltpu.SemaphoreType.DMA((copies,)),
+        ],
+        compiler_params=pltpu.CompilerParams(
+            collective_id=1, has_side_effects=True, vmem_limit_bytes=48 * 1024 * 1024
+        ),
+    )(wg.reshape((rows, 2 * in_ch)))
+    return up, ig, total.transpose(0, 1, 2, 4, 3)
 
 
 def solution(mesh):

time: 208 us -> 76.3 us (0.37)
  waiting for transfers between devices: 134 us -> 0 us
  Pallas kernels: 6.68 us -> 67 us
  starting transfers between devices: 19.7 us -> 0 us
  local copies, waits for them, and re-layouts: 26.8 us -> 8.44 us
  between operations: 14.4 us -> 0.67 us
  other arithmetic: 6.22 us -> 0 us
    psum x1 -> x0, waiting for transfers between devices: 124 us -> none  [body(): total = lax.psum(wg, ('gx', 'gy', 'gz'))]
    pallas_call x0 -> x2, Pallas kernels: none -> 60.1 us  [the longest x1 31.2 us: body(): pl.pallas_call(functools.partial(reduce_kernel, plan, 1.0 / math.sqrt(all...]
    ppermute x12 -> x0, starting transfers between devices: 19.6 us -> none  [the longest x8 11 us: ring(): lax.ppermute(value, axis, [(i, (i + step) % count) for i in range(count)])]
    ppermute x12 -> x0, waiting for transfers between devices: 9.73 us -> none  [the longest x8 5.43 us: ring(): lax.ppermute(value, axis, [(i, (i + step) % count) for i in range(count)])]
    slice x12 -> x0, local copies, waits for them, and re-layouts: 8.18 us -> none  [the longest x1 2.14 us: body(): grads[:, :, :, :out_ch, 0]]
    unnamed x24 -> x5, local copies, waits for them, and re-layouts: 10.2 us -> 3.36 us
    reshape x6 -> x0, local copies, waits for them, and re-layouts: 4.14 us -> none  [the longest x1 1.65 us: body(): total.reshape((2, 2, 2, 2, 2, out_ch, 2, in_ch))]
    concatenate x8 -> x0, other arithmetic: 3.54 us -> none  [the longest x1 1.35 us: body(): jnp.concatenate([ring(cells[:, -1:], 'gy', 1), cells, ring(cells[:, :1],...]
  transfers between devices with their start and end apart: 13 -> 0, of which waited for: 5 -> 0; matrix products, arithmetic and copies ran while one was open for 11% -> 0% of each run, Pallas kernels for 0% -> 0%
where the time goes in v1:
time: 76.3 us; the launch traced here: 76.1 us
  Pallas kernels  67 us (88%)
  local copies, waits for them, and re-layouts  8.44 us (11%)
    pallas_call x1, Pallas kernels, body(): pl.pallas_call(functools.partial(reduce_kernel, plan, 1.0 / math.sqrt(all...  31.2 us
    pallas_call x1, Pallas kernels, body(): pl.pallas_call(halo_kernel, out_shape=(jax.ShapeDtypeStruct((cells_x + 2,...  28.9 us
    pallas_call x1, Pallas kernels, body(): pl.pallas_call(compute_kernel, out_shape=(jax.ShapeDtypeStruct((cells_x,...  6.91 us
    unnamed x5, local copies, waits for them, and re-layouts  3.36 us
    reshape x1, local copies, waits for them, and re-layouts, body(): up.reshape((cells_x, cells_y, 2, 2, 2, out_ch, cells_z))  2.67 us
    transpose x1, local copies, waits for them, and re-layouts, body(): cotangent.transpose(4, 5, 0, 1, 2, 3, 6)  2.4 us

profile of v1, /device:TPU:0, one launch (start us, length us, event | category | flops | bytes accessed | tf_op | source)
XLA Modules:
  0.0 76.1 jit_solution(17685423418464656711)
XLA Ops:
  0.6 1.2 %copy.13 = bf16[64,4,8,128]{3,0,2,1:T(8,128)(2,1)S(1)} copy(bf16[64,4,8,128]{3,2,1,0:T(8,128)(2,1)} %param.3) | data formatting | bytes 1048576 | tf_op args[0]
  1.9 2.4 %copy.7 = bf16[4,8,2,2,2,32,128]{6,5,4,3,2,1,0:T(8,128)(2,1)S(1)} copy(bf16[4,8,2,2,2,32,128]{6,1,0,5,4,3,2:T(8,128)(2,1)} %bitcast.22) | data formatting | bytes 4194304 | tf_op jit(solution)/shard_map/transpose | solution.py:444
  4.3 0.0 copy-start
  4.3 28.9 %shard_map.58 = (bf16[6,10,64,128]{3,2,1,0:T(8,128)(2,1)S(1)}, bf16[5,9,4,64,128]{4,3,2,1,0:T(8,128)(2,1)}, bf16[2,64,128]{2,1,0:T(8,128)(2,1)S(1)}, bf16[2,128,128]{2,1,0:T(8,128)(2,1)S(1)}) custom-call(bf16[4,8,64,128]{3,2,1,0:T(8,128)(2,1)S(1)} %bitcast.16, bf16[4,8,4,64,128]{4,3,2,1,0:T(8,128)(2,1)S(1)} %bitcast.14), custom_call_target="tpu_custom_call" | custom-call | tf_op jit(solution)/shard_map/pallas_call | solution.py:449
  33.2 0.0 copy-done
  33.2 6.9 %shard_map.59 = (bf16[4,8,4,64,128]{4,3,2,1,0:T(8,128)(2,1)S(1)}, bf16[4,8,64,128]{3,2,1,0:T(8,128)(2,1)S(1)}, f32[2,512,128]{2,1,0:T(8,128)S(1)}) custom-call(bf16[6,10,64,128]{3,2,1,0:T(8,128)(2,1)S(1)} %get-tuple-element.10.in_ref, bf16[5,9,4,64,128]{4,3,2,1,0:T(8,128)(2,1)} %get-tuple-element.11.g_ref, ...), custom_call_target="tpu_custom_call" | custom-call | tf_op jit(solution)/shard_map/pallas_call | solution.py:471
  40.1 2.7 %copy.12 = bf16[4,8,2,2,2,32,128]{6,1,0,5,4,3,2:T(8,128)(2,1)} copy(bf16[4,8,2,2,2,32,128]{6,5,4,3,2,1,0:T(8,128)(2,1)S(1)} %bitcast.17) | data formatting | bytes 4194304 | tf_op jit(solution)/shard_map/reshape | solution.py:486
  42.8 1.1 %copy.9 = bf16[64,4,8,128]{3,2,1,0:T(8,128)(2,1)} copy(bf16[64,4,8,128]{3,0,2,1:T(8,128)(2,1)S(1)} %bitcast.20) | data formatting | bytes 1048576
  43.9 31.2 %shard_map.60 = f32[4,4,4,32,64]{4,3,2,1,0:T(8,128)S(1)} custom-call(f32[1024,128]{1,0:T(8,128)S(1)} %bitcast.19), custom_call_target="tpu_custom_call" | custom-call | tf_op jit(solution)/shard_map/pallas_call | solution.py:499
  75.1 1.0 %copy.15 = f32[4,4,4,64,32]{3,4,2,1,0:T(8,128)} copy(f32[4,4,4,64,32]{3,4,2,1,0:T(8,128)S(1)} %bitcast.15) | data formatting | bytes 1048576
Async XLA Ops:
  4.3 28.9 %copy-start = (bf16[4,4,4,64,32]{3,4,2,1,0:T(8,128)(2,1)S(1)}, bf16[4,4,4,64,32]{3,4,2,1,0:T(8,128)(2,1)}, u32[]{:S(2)}) copy-start(bf16[4,4,4,64,32]{3,4,2,1,0:T(8,128)(2,1)} %param.4) | copy-start | bytes 786436
